TPU v7x, 256 devices: a whole 4x4x8 slice. The times are simulated.
256 devices in a mesh: img: 8 (over z), cls: 32 (over x, y, core).
Axes of the slice: x: 4, y: 4, z: 8, core: 2. Of those that a mesh axis runs over, the one named last changes fastest.
Arguments:
- picture_token_states: bfloat16 [8192, 1664], P(('img', 'cls')), may hold values from -6 to 90
- layer_scaling_coefficients: float32 [1664], replicated, may hold values from 0.5 to 1.5
- expanding_linear_map: bfloat16 [1664, 8192], P(None, 'cls'), may hold values from -0.15625 to 0.15625
- contracting_linear_map: bfloat16 [8192, 1664], P('cls'), may hold values from -0.0625 to 0.0625
- closing_scaling_coefficients: float32 [1664], replicated, may hold values from 0.5 to 1.5
- joint_space_mapper: bfloat16 [1664, 1280], replicated, may hold values from -0.0501 to 0.0501
- prompt_caption_encodings: bfloat16 [16384, 16, 1280], P('cls', 'img'), may hold values from -6 to 6
- prompt_category_multiplicity: int32 [16384, 16], P('cls'), may hold values from 1 to 9
- sharpness_multiplier: float32 [1], replicated, may hold values from 280 to 420
Outputs:
- log_probs: float32 [8192, 16384], P('img', 'cls')
All inputs are finite; a program needn't handle non-finite values.
Results may differ from a plain program's by a relative error of at most 0.0059.
Values may be sent and summed in bfloat16 or wider, within the bound.
A program may use at most 64 MiB of HBM per device.

v0:
```python
import jax
import jax.numpy as jnp
from jax import lax
from jax.sharding import PartitionSpec as P

epsilon = 1e-05


def layer_norm(values, gain_vec):
    center = values - jnp.mean(values, axis=-1, keepdims=True)
    variance = jnp.mean(center * center, axis=-1, keepdims=True)
    return center * lax.rsqrt(variance + epsilon) * gain_vec


def embed_rows(stream, closing_scaling_coefficients, joint_space_mapper):
    pooled = layer_norm(stream, closing_scaling_coefficients).astype(jnp.bfloat16)
    projected = jnp.dot(pooled, joint_space_mapper, preferred_element_type=jnp.float32)
    return (
        projected * lax.rsqrt(jnp.sum(projected * projected, axis=-1, keepdims=True) + 1e-06)
    ).astype(jnp.bfloat16)


def rounded_term(values):
    return lax.optimization_barrier(values.astype(jnp.bfloat16)).astype(jnp.float32)


def shards(
    picture_token_states,
    layer_scaling_coefficients,
    expanding_linear_map,
    contracting_linear_map,
    closing_scaling_coefficients,
    joint_space_mapper,
    prompt_caption_encodings,
    prompt_category_multiplicity,
    sharpness_multiplier,
):
    gathered = lax.all_gather(picture_token_states, "cls", axis=0, tiled=True)
    residual = gathered.astype(jnp.float32)
    normed = layer_norm(residual, layer_scaling_coefficients).astype(jnp.bfloat16)
    hidden = jax.nn.gelu(
        jnp.dot(normed, expanding_linear_map, preferred_element_type=jnp.float32), approximate=False
    ).astype(jnp.bfloat16)
    own_sum = lax.psum_scatter(
        rounded_term(
            jnp.dot(hidden, contracting_linear_map, preferred_element_type=jnp.float32)
        ).astype(jnp.bfloat16),
        "cls",
        scatter_dimension=0,
        tiled=True,
    ).astype(jnp.float32)
    own_embedding = embed_rows(
        picture_token_states.astype(jnp.float32) + own_sum,
        closing_scaling_coefficients,
        joint_space_mapper,
    )
    joint_space_features = lax.all_gather(own_embedding, "cls", axis=0, tiled=True)
    tpl_count = prompt_caption_encodings.shape[1]
    weights_f = prompt_category_multiplicity.astype(jnp.float32)
    offset = lax.axis_index("img") * tpl_count
    own_weights = lax.dynamic_slice_in_dim(weights_f, offset, tpl_count, 1)
    portion = own_weights / jnp.sum(weights_f, axis=1, keepdims=True)
    tmpl = prompt_caption_encodings.astype(jnp.float32)
    unit_templates = tmpl * lax.rsqrt(jnp.sum(tmpl * tmpl, axis=-1, keepdims=True) + 1e-06)
    group_sum = rounded_term(jnp.einsum("ct,cte->ce", portion, unit_templates))
    blended = lax.psum(group_sum.astype(jnp.bfloat16), "img")
    category_affinity_values = (
        lax.dot_general(
            joint_space_features,
            blended,
            (((1,), (1,)), ((), ())),
            preferred_element_type=jnp.float32,
        )
        * sharpness_multiplier[0]
    )
    local_max = jnp.max(category_affinity_values, axis=1, keepdims=True)
    row_max = lax.pmax(local_max, "cls")
    row_total = lax.psum(
        jnp.sum(jnp.exp(category_affinity_values - row_max), axis=1, keepdims=True), "cls"
    )
    return category_affinity_values - row_max - jnp.log(row_total)


def solution(mesh):
    in_specs = (
        P(("img", "cls"), None),
        P(),
        P(None, "cls"),
        P("cls", None),
        P(),
        P(),
        P("cls", "img", None),
        P("cls", None),
        P(),
    )
    out_specs = P("img", "cls")
    return jax.shard_map(shards, mesh=mesh, in_specs=in_specs, out_specs=out_specs, check_vma=False)
```

profile of v0, /device:TPU:1, one launch (start us, length us, event | category | flops | bytes accessed | tf_op | source)
XLA Modules:
  0.0 365.0 jit_solution(11576788650239403848)
XLA Ops:
  7.4 0.7 all-gather.3.cloned.1.call-update
  8.1 57.2 %all-gather.3.cloned.1.call-done = bf16[1024,1664]{1,0:T(8,128)(2,1)} async-done(((bf16[32,1664]{1,0:T(8,128)(2,1)}), bf16[1024,1664]{1,0:T(8,128)(2,1)}) %all-gather.3.cloned.1.call-update) | async-done | bytes 3407888 | tf_op jit(solution)/shard_map/all_gather | solution.py:38
  65.3 2.6 convert_reduce_fusion
  68.0 0.3 copy-done.1
  68.3 1.0 fusion.2
  69.4 9.1 %convolution_convert_fusion = bf16[1024,1664]{1,0:T(8,128)(2,1)} fusion(bf16[256,1664]{1,0:T(8,128)(2,1)S(1)} %copy-done, bf16[1664,256]{1,0:T(8,128)(2,1)S(1)} %copy-done.7, bf16[1024,1664]{1,0:T(8,128)(2,1)} %all-gather.3.cloned.1.call-done, f32[1664]{0:T(1024)S(1)} %copy-done.8, f32[1024]{0:T(1024)S(1)} %add_rsqrt_fusion.1, ...), kind=kOutput, calls=%fused_computation.11 | convolution fusion | flops 1772093440 | bytes 8534528 | tf_op jit(solution)/shard_map/dot_general | solution.py:46
  78.6 0.7 copy-done.5
  79.3 0.9 copy.12
  80.2 0.0 copy-done.2
  80.2 2.8 fusion.5
  83.1 4.4 %fusion.6 = bf16[512,1,1280]{2,1,0:T(2,128)(2,1)} fusion(bf16[512,2,1]{1,2,0:T(2,128)(2,1)S(1)} %copy-done.4, bf16[512,2,1280]{2,1,0:T(2,128)(2,1)S(1)} %copy-done.2, f32[512,2]{1,0:T(8,128)S(1)} %add_rsqrt_fusion), kind=kOutput, calls=%fused_computation.10 | convolution fusion | flops 5242880 | bytes 3938304 | tf_op jit(solution)/shard_map/ct,cte->ce/dot_general | solution.py:65
  87.5 3.1 copy.15
  90.6 74.3 %reduce-scatter.2.cloned.1.call-done = bf16[32,1664]{1,0:T(8,128)(2,1)} async-done(((bf16[1024,1664]{1,0:T(8,128)(2,1)}), bf16[32,1664]{1,0:T(8,128)(2,1)}) %reduce-scatter.2.cloned.1.call-update) | async-done | bytes 106512 | tf_op jit(solution)/shard_map/reduce_scatter | solution.py:44
  164.9 1.0 fusion.58
  166.0 1.1 multiply_reduce_fusion.1
  167.1 3.1 multiply_reduce_fusion.2
  170.2 0.7 multiply_convert_fusion.1
  171.6 50.1 %all-gather.5.cloned.1.call-done = bf16[1024,1280]{1,0:T(8,128)(2,1)} async-done(((bf16[32,1280]{1,0:T(8,128)(2,1)}), bf16[1024,1280]{1,0:T(8,128)(2,1)}) %all-gather.5.cloned.1.call-update) | async-done | bytes 2621456 | tf_op jit(solution)/shard_map/all_gather | solution.py:57
  221.8 3.7 %multiply_reduce_fusion = (f32[1024]{0:T(1024)S(1)}, f32[1024,512]{0,1:T(8,128)S(1)}) fusion(f32[]{:T(128)} %bitcast.14, bf16[1024,1280]{1,0:T(8,128)(2,1)} %all-gather.5.cloned.1.call-done, bf16[512,1280]{1,0:T(8,128)(2,1)} %all-reduce.2.cloned.1.call-done), kind=kOutput, calls=%fused_computation.20 | convolution fusion | flops 1343224832 | bytes 6033412 | tf_op jit(solution)/shard_map/dot_general | solution.py:68
  225.5 62.3 %pmax.7 = f32[1024]{0:T(1024)S(1)} all-reduce(f32[1024]{0:T(1024)S(1)} %get-tuple-element.7), channel_id=1, replica_groups=mesh['img'=8,'cls'=32] {'cls'}, use_global_device_ids=true, to_apply=%region_10.0 | all-reduce | flops 1024 | bytes 8192 | tf_op jit(solution)/shard_map/pmax | solution.py:77
  287.7 0.4 exponential_reduce_fusion
  288.1 65.2 %psum.15 = f32[1024,1]{0,1:T(1,128)S(1)} all-reduce(f32[1024,1]{0,1:T(1,128)S(1)} %bitcast.18), channel_id=1, replica_groups=mesh['img'=8,'cls'=32] {'cls'}, use_global_device_ids=true, to_apply=%region_12.0 | all-reduce | flops 1024 | bytes 8192 | tf_op jit(solution)/shard_map/psum | solution.py:78
  353.3 1.7 subtract_subtract_fusion
  355.0 2.9 copy.11
  (33 shorter events, 0.4 us)
Async XLA Ops:
  7.4 62.0 %copy-start = (bf16[256,1664]{1,0:T(8,128)(2,1)S(1)}, bf16[256,1664]{1,0:T(8,128)(2,1)}, u32[]{:S(2)}) copy-start(bf16[256,1664]{1,0:T(8,128)(2,1)} %param.12) | copy-start | bytes 2555908
  7.4 58.0 %all-gather.3.cloned.1.call-start = ((), (), s32[]{:S(2)}) async-start(), calls=%async_computation.1 | async-start | bytes 3514368 | tf_op jit(solution)/shard_map/all_gather | solution.py:38
  8.1 61.3 %copy-start.8 = (f32[1664]{0:T(1024)S(1)}, f32[1664]{0:T(1024)}, u32[]{:S(2)}) copy-start(f32[1664]{0:T(1024)} %param.10) | copy-start | bytes 19972
  8.1 156.8 %reduce-scatter.2.cloned.1.call-start = ((), (), s32[]{:S(2)}) async-start(), calls=%async_computation.2 | async-start | bytes 3514368 | tf_op jit(solution)/shard_map/reduce_scatter | solution.py:44
  65.3 3.0 copy-start.1
  65.3 4.1 %copy-start.7 = (bf16[1664,256]{1,0:T(8,128)(2,1)S(1)}, bf16[1664,256]{1,0:T(8,128)(2,1)}, u32[]{:S(2)}) copy-start(bf16[1664,256]{1,0:T(8,128)(2,1)} %param.11) | copy-start | bytes 2555908
  78.5 0.8 copy-start.5
  78.5 1.8 copy-start.2
  78.5 93.1 %all-reduce.2.cloned.1.call-start = ((), (), s32[]{:S(2)}) async-start(), calls=%async_computation.4 | async-start | bytes 2621440 | tf_op jit(solution)/shard_map/psum | solution.py:66
  80.2 2.8 copy-start.4
  87.5 77.4 %copy-start.3 = (bf16[32,1664]{1,0:T(8,128)(2,1)S(1)}, bf16[32,1664]{1,0:T(8,128)(2,1)}, u32[]{:S(2)}) copy-start(bf16[32,1664]{1,0:T(8,128)(2,1)} %param.9) | copy-start | bytes 319492
  87.5 79.6 %copy-start.6 = (f32[1664]{0:T(1024)S(1)}, f32[1664]{0:T(1024)}, u32[]{:S(2)}) copy-start(f32[1664]{0:T(1024)} %param.13) | copy-start | bytes 19972
  90.6 131.2 %all-gather.5.cloned.1.call-start = ((), (), s32[]{:S(2)}) async-start(), calls=%async_computation.3 | async-start | bytes 2703360 | tf_op jit(solution)/shard_map/all_gather | solution.py:57
Sparse Core Ops, SparseCore 0:
  10.7 54.5 all-gather.2
  78.6 86.2 reduce-scatter.1
  171.1 50.6 all-gather.4
Sparse Core Ops, SparseCore 1:
  90.7 71.7 all-reduce.1
where the time goes:
time: 365 us
  waiting for transfers between devices  182 us (50%)
  blocking collectives  127 us (35%)
  matrix products  20.3 us (6%)
  between operations  15.3 us (4%)
  other arithmetic  11.4 us (3%)
  local copies, waits for them, and re-layouts  7.98 us (2%)
    reduce_scatter x1, waiting for transfers between devices, shards(): lax.psum_scatter(rounded_term(jnp.dot(hidden, contracting_linear_map, pre...  74.3 us
    psum x1, blocking collectives, shards(): lax.psum(jnp.sum(jnp.exp(category_affinity_values - row_max), axis=1, kee...  65.2 us
    pmax x1, blocking collectives, shards(): row_max = lax.pmax(local_max, 'cls')  62.3 us
    all_gather x1, waiting for transfers between devices, shards(): gathered = lax.all_gather(picture_token_states, 'cls', axis=0, tiled=True)  57.2 us
    all_gather x1, waiting for transfers between devices, shards(): lax.all_gather(own_embedding, 'cls', axis=0, tiled=True)  50.1 us
    dot_general x1, matrix products, shards(): jnp.dot(hidden, contracting_linear_map, preferred_element_type=jnp.float32)  9.09 us
  transfers between devices with their start and end apart: 4, of which 3 were waited for; matrix products, arithmetic and copies ran while one was open for 5% of the time, Pallas kernels for 0%

commit v1 on v0

v1 whole, which is shorter than its diff:
```python
import jax
import jax.numpy as jnp
from jax import lax
from jax.experimental import pallas as pl
from jax.experimental.pallas import tpu as pltpu
from jax.sharding import PartitionSpec as P

MESH = pl.DeviceIdType.MESH
F32 = jnp.float32
BF16 = jnp.bfloat16
ORDER = (1, 3, 2)


def layer_norm(values, gain):
    center = values - jnp.mean(values, axis=-1, keepdims=True)
    variance = jnp.mean(center * center, axis=-1, keepdims=True)
    return center * lax.rsqrt(variance + 1e-05) * gain


def arrived(ref, sem):
    pltpu.make_async_copy(ref, ref, sem).wait()


class PlaneGather:
    def __init__(self, x, y, at, buf, sems):
        self.x, self.y, self.at, self.buf = x, y, at, buf
        self.a1, self.a2, self.b1, self.b2, self.out = sems

    def send(self, h, xx, yy, to, sem):
        piece = self.buf.at[h, xx * 4 + yy]
        pltpu.make_async_remote_copy(
            src_ref=piece, dst_ref=piece, send_sem=self.out, recv_sem=sem, device_id=to, device_id_type=MESH
        ).start()

    def start(self):
        x, y = self.x, self.y
        for d in ORDER:
            self.send(0, x, y, self.at((x + d) % 4, y), self.a1.at[4 - d])
            self.send(1, x, y, self.at(x, (y + d) % 4), self.b1.at[4 - d])
        for d in ORDER:
            self.send(0, x, y, self.at(x, (y + d) % 4), self.a2.at[0])
            self.send(1, x, y, self.at((x + d) % 4, y), self.b2.at[4 - d])

    def forward(self):
        x, y = self.x, self.y
        for o in ORDER:
            xs, ys = (x + o) % 4, (y + o) % 4
            arrived(self.buf.at[0, xs * 4 + y], self.a1.at[o])
            for d in ORDER:
                self.send(0, xs, y, self.at(x, (y + d) % 4), self.a2.at[o])
            arrived(self.buf.at[1, x * 4 + ys], self.b1.at[o])
            for d in ORDER:
                self.send(1, x, ys, self.at((x + d) % 4, y), self.b2.at[4 - d])

    def column(self, o):
        arrived(self.buf.at[0, pl.ds(0, 3)], self.a2.at[o])
        if o:
            arrived(self.buf.at[1, pl.ds(0, 4)], self.b2.at[o])

    def finish(self):
        arrived(self.buf.at[:, pl.ds(0, 15)], self.out)


def kernel(
    x_ref, g1_ref, w1_hbm, w2_hbm, g2_ref, map_hbm, tpl_hbm, mult_ref, sharp_ref,
    logit_out, lse_out,
    tok, w1, w2, part, r1a, r1b, s1a, s1b, r2a, r2b, mapv, emb, tplv, shc, gs, zr, zs, cls, lg, lse_mine, lse_in,
    load_sem, w_send, w_recv, g_a1, g_a2, g_b1, g_b2, g_out, e_a1, e_a2, e_b1, e_b2, e_out,
    ra1, rb1, ra2, rb2, rs_out, z_recv, z_out, za_recv, za_out, pair_recv, pair_out, lo_sem, l_recv, l_out,
):
    m = lax.axis_index("cls")
    z = lax.axis_index("img")
    x, y, c = m // 8, (m // 2) % 4, m % 2
    me = x * 4 + y

    def at(xx, yy):
        return (z, (xx * 4 + yy) * 2 + c)

    mate = (z, me * 2 + (1 - c))
    z_up, z_down = ((z + 1) % 8, m), ((z + 7) % 8, m)

    def send(src, dst, s_sem, r_sem, to):
        pltpu.make_async_remote_copy(
            src_ref=src, dst_ref=dst, send_sem=s_sem, recv_sem=r_sem, device_id=to, device_id_type=MESH
        ).start()

    barrier = pltpu.get_barrier_semaphore()
    partners = [at((x + d) % 4, y) for d in ORDER] + [at(x, (y + d) % 4) for d in ORDER] + [mate, z_up, z_down]
    for to in partners:
        pl.semaphore_signal(barrier, inc=1, device_id=to, device_id_type=MESH)

    loads = [
        pltpu.make_async_copy(tpl_hbm, tplv, load_sem.at[0]),
        pltpu.make_async_copy(w1_hbm, w1.at[c], load_sem.at[1]),
        pltpu.make_async_copy(w2_hbm, w2.at[c], load_sem.at[2]),
        pltpu.make_async_copy(map_hbm, mapv, load_sem.at[3]),
    ]
    for load in loads:
        load.start()

    states = x_ref[...].astype(F32)
    normed = layer_norm(states, g1_ref[...][None, :]).astype(BF16)
    tok[0, me] = normed[:16]
    tok[1, me] = normed[16:]

    pl.semaphore_wait(barrier, len(partners))

    gather = PlaneGather(x, y, at, tok, (g_a1, g_a2, g_b1, g_b2, g_out))
    gather.start()
    send(w1_hbm, w1.at[c], w_send.at[0], w_recv.at[0], mate)
    send(w2_hbm, w2.at[c], w_send.at[1], w_recv.at[1], mate)

    weights = mult_ref[...].astype(F32)
    total = jnp.sum(weights, axis=0, keepdims=True)
    row_id = lax.broadcasted_iota(jnp.int32, weights.shape, 0)
    for t in range(2):
        own = jnp.sum(jnp.where(row_id == 2 * z + t, weights, 0.0), axis=0, keepdims=True)
        portion = own / total
        for q in range(4):
            shc[t, pl.ds(q * 128, 128), :] = jnp.broadcast_to(portion[:, q * 128 : (q + 1) * 128], (128, 128)).T

    def group_sums(lo, hi):
        @pl.loop(lo, hi)
        def _(k):
            for i in range(2):
                rows = pl.ds(k * 64 + i * 32, 32)
                acc = None
                for t in range(2):
                    tmpl = tplv[t, rows, :].astype(F32)
                    coef = shc[t, rows, 0:1] * lax.rsqrt(jnp.sum(tmpl * tmpl, axis=-1, keepdims=True) + 1e-06)
                    acc = coef * tmpl if acc is None else acc + coef * tmpl
                gs[k, pl.ds(i * 32, 32), :] = acc.astype(BF16)

    loads[0].wait()
    group_sums(0, 4)
    gather.forward()
    group_sums(4, 8)

    halves = (pl.ds(0, 640), pl.ds(640, 640))

    def z_reduce(s):
        for way, half in ((0, 0), (1, 1), (0, 1), (1, 0)):
            if s == 0 and way != half:
                continue
            cols = halves[half]
            k = (z + 4 + s) % 8 if way == 0 else (z + 4 - s + 8) % 8
            first = s == 0 or (s == 1 and way != half)
            if first:
                src = gs.at[k, :, cols]
            else:
                came = zr.at[way, s - 1, :, cols]
                arrived(came, z_recv.at[way, half, s - 1])
                zs[way, s, :, cols] = (gs[k, :, cols].astype(F32) + came[...].astype(F32)).astype(BF16)
                src = zs.at[way, s, :, cols]
            send(src, zr.at[way, s, :, cols], z_out, z_recv.at[way, half, s], z_down if way == 0 else z_up)

    def z_total():
        for half in range(2):
            cols = halves[half]
            for way in range(2):
                arrived(zr.at[way, 3, :, cols], z_recv.at[way, half, 3])
            cls[z, :, cols] = (
                gs[z, :, cols].astype(F32) + zr[0, 3, :, cols].astype(F32) + zr[1, 3, :, cols].astype(F32)
            ).astype(BF16)

    def z_gather(s):
        for way, half in ((0, 0), (1, 1), (0, 1), (1, 0)):
            cols = halves[half]
            far = 4 if way == half else 3
            k = (z + s) % 8 if way == 0 else (z - s + 8) % 8
            if s > far:
                continue
            chunk = cls.at[k, :, cols]
            if s > 0:
                arrived(chunk, za_recv.at[way, half, s - 1])
            if s < far:
                send(chunk, chunk, za_out, za_recv.at[way, half, s], z_down if way == 0 else z_up)

    z_reduce(0)

    def ffn(o):
        xs = (x + o) % 4
        gather.column(o)
        rows = tok[:, pl.ds(xs * 4, 4)].reshape(128, tok.shape[-1])
        out = None
        for k in range(2):
            pre = jnp.dot(rows, w1[k], preferred_element_type=F32)
            hidden = (pre * 0.5 * (1.0 + lax.erf(pre * 0.7071067811865476))).astype(BF16)
            term = jnp.dot(hidden, w2[k], preferred_element_type=F32)
            out = term if out is None else out + term
        part[:, pl.ds(xs * 4, 4)] = out.astype(BF16).reshape(2, 4, 16, tok.shape[-1])
        for d in ORDER:
            yd = (y + d) % 4
            send(part.at[0, xs * 4 + yd], r1a.at[3 - d, o], rs_out.at[0], ra1.at[o], at(x, yd))
        if o:
            send(part.at[1, pl.ds(xs * 4, 4)], r1b.at[3 - o], rs_out.at[1], rb1.at[3 - o], at(xs, y))

    loads[1].wait()
    loads[2].wait()
    arrived(w1.at[1 - c], w_recv.at[0])
    arrived(w2.at[1 - c], w_recv.at[1])
    ffn(0)
    z_reduce(1)
    ffn(1)
    ffn(3)
    z_reduce(2)
    ffn(2)

    for o in ORDER:
        xs = (x + o) % 4
        arrived(r1a.at[:, o], ra1.at[o])
        s1a[o] = (
            part[0, xs * 4 + y].astype(F32) + r1a[0, o].astype(F32) + r1a[1, o].astype(F32) + r1a[2, o].astype(F32)
        ).astype(BF16)
        send(s1a.at[o], r2a.at[3 - o], rs_out.at[2], ra2.at[0], at(xs, y))
    z_reduce(3)
    for k in range(3):
        arrived(r1b.at[k], rb1.at[k])
    for o in ORDER:
        ys = (y + o) % 4
        s1b[o] = (
            part[1, x * 4 + ys].astype(F32) + r1b[0, ys].astype(F32) + r1b[1, ys].astype(F32) + r1b[2, ys].astype(F32)
        ).astype(BF16)
        send(s1b.at[o], r2b.at[3 - o], rs_out.at[3], rb2.at[0], at(x, ys))
    arrived(r1a.at[:, 0], ra1.at[0])
    own_a = part[0, me].astype(F32) + r1a[0, 0].astype(F32) + r1a[1, 0].astype(F32) + r1a[2, 0].astype(F32)
    own_b = part[1, me].astype(F32) + r1b[0, y].astype(F32) + r1b[1, y].astype(F32) + r1b[2, y].astype(F32)
    gather.finish()
    arrived(r2a, ra2.at[0])
    arrived(r2b, rb2.at[0])
    for k in range(3):
        own_a = own_a + r2a[k].astype(F32)
        own_b = own_b + r2b[k].astype(F32)
    stream = states + jnp.concatenate([own_a, own_b], axis=0)
    pooled = layer_norm(stream, g2_ref[...][None, :]).astype(BF16)
    loads[3].wait()
    projected = jnp.dot(pooled, mapv[...], preferred_element_type=F32)
    embedding = (
        projected * lax.rsqrt(jnp.sum(projected * projected, axis=-1, keepdims=True) + 1e-06)
    ).astype(BF16)
    emb[c, 0, me] = embedding[:16]
    emb[c, 1, me] = embedding[16:]
    spread = PlaneGather(x, y, at, emb.at[c], (e_a1, e_a2, e_b1, e_b2, e_out))
    spread.start()
    z_total()
    z_gather(0)
    spread.forward()
    z_gather(1)
    z_gather(2)
    z_gather(3)
    z_gather(4)

    sharp = sharp_ref[0]

    def logits(core, o):
        xs = (x + o) % 4
        rows = emb[core, :, pl.ds(xs * 4, 4)].reshape(128, emb.shape[-1])
        classes = cls[...].reshape(512, emb.shape[-1])
        val = sharp * lax.dot_general(rows, classes, (((1,), (1,)), ((), ())), preferred_element_type=F32)
        for h in range(2):
            for yy in range(4):
                lo = h * 64 + yy * 16
                lg[xs * 4 + yy, core, h] = val[lo : lo + 16]
        pltpu.make_async_copy(lg.at[pl.ds(xs * 4, 4), core], logit_out.at[pl.ds(xs * 4, 4), core], lo_sem).start()
        top = jnp.max(val, axis=-1, keepdims=True)
        lse = top + jnp.log(jnp.sum(jnp.exp(val - top), axis=-1, keepdims=True))
        lse_mine[0, pl.ds(core * 4 + xs, 1), :] = jnp.broadcast_to(lse, (128, 128)).T[0:1, :]

    def own_column(o):
        spread.column(o)
        quad = emb.at[c, :, pl.ds(((x + o) % 4) * 4, 4)]
        send(quad, quad, pair_out, pair_recv.at[o], mate)

    def mate_column(o):
        arrived(emb.at[1 - c, :, pl.ds(((x + o) % 4) * 4, 4)], pair_recv.at[o])

    own_column(0)
    logits(c, 0)
    own_column(1)
    logits(c, 1)
    mate_column(0)
    logits(1 - c, 0)
    own_column(3)
    logits(c, 3)
    mate_column(1)
    logits(1 - c, 1)
    own_column(2)
    logits(c, 2)
    mate_column(3)
    logits(1 - c, 3)
    mate_column(2)
    logits(1 - c, 2)

    def merge(values):
        top = values[0]
        for v in values[1:]:
            top = jnp.maximum(top, v)
        acc = jnp.exp(values[0] - top)
        for v in values[1:]:
            acc = acc + jnp.exp(v - top)
        return top + jnp.log(acc)

    send(lse_mine.at[0], lse_in.at[0], l_out.at[0], l_recv.at[0], mate)
    arrived(lse_in.at[0], l_recv.at[0])
    lse_mine[1] = merge([lse_mine[0], lse_in[0]])
    for d in ORDER:
        send(lse_mine.at[1], lse_in.at[4 - d], l_out.at[1], l_recv.at[4 - d], at((x + d) % 4, y))
    for d in ORDER:
        arrived(lse_in.at[d], l_recv.at[d])
    lse_mine[2] = merge([lse_mine[1]] + [lse_in[d] for d in ORDER])
    for d in ORDER:
        send(lse_mine.at[2], lse_in.at[3 + 4 - d], l_out.at[2], l_recv.at[3 + 4 - d], at(x, (y + d) % 4))

    spread.finish()
    arrived(w1.at[c], w_send.at[0])
    arrived(w2.at[c], w_send.at[1])
    arrived(part.at[0, pl.ds(0, 12)], rs_out.at[0])
    arrived(part.at[0, pl.ds(0, 12)], rs_out.at[1])
    arrived(r2a, rs_out.at[2])
    arrived(r2b, rs_out.at[3])
    arrived(gs.at[pl.ds(0, 7)], z_out)
    arrived(gs.at[pl.ds(0, 7)], za_out)
    arrived(emb.at[c], pair_out)
    arrived(lg, lo_sem)
    arrived(lse_in.at[0], l_out.at[0])
    arrived(lse_in.at[pl.ds(0, 3)], l_out.at[1])

    for d in ORDER:
        arrived(lse_in.at[3 + d], l_recv.at[3 + d])
    lse = merge([lse_mine[2]] + [lse_in[3 + d] for d in ORDER])
    for q in range(8):
        columns = jnp.broadcast_to(lse[q : q + 1, :], (128, 128)).T
        for h in range(2):
            for yy in range(4):
                lo = h * 64 + yy * 16
                lse_out[(q % 4) * 4 + yy, q // 4, h] = columns[lo : lo + 16]
    arrived(lse_in.at[pl.ds(0, 3)], l_out.at[2])


def shards(states, gain1, w1, w2, gain2, mapper, prompts, multiplicity, sharpness):
    width = states.shape[1]
    edim = mapper.shape[1]
    vmem = pl.BlockSpec(memory_space=pltpu.VMEM)
    anywhere = pl.BlockSpec(memory_space=pl.ANY)
    dma = pltpu.SemaphoreType.DMA
    logit, lse = pl.pallas_call(
        kernel,
        name="whole",
        out_shape=(
            jax.ShapeDtypeStruct((16, 2, 2, 16, 512), F32),
            jax.ShapeDtypeStruct((16, 2, 2, 16, 128), F32),
        ),
        in_specs=[vmem, vmem, anywhere, anywhere, vmem, anywhere, anywhere, vmem, pl.BlockSpec(memory_space=pltpu.SMEM)],
        out_specs=(anywhere, vmem),
        scratch_shapes=[
            pltpu.VMEM((2, 16, 16, width), BF16),
            pltpu.VMEM((2, width, 256), BF16),
            pltpu.VMEM((2, 256, width), BF16),
            pltpu.VMEM((2, 16, 16, width), BF16),
            pltpu.VMEM((3, 4, 16, width), BF16),
            pltpu.VMEM((3, 4, 16, width), BF16),
            pltpu.VMEM((4, 16, width), BF16),
            pltpu.VMEM((4, 16, width), BF16),
            pltpu.VMEM((3, 16, width), BF16),
            pltpu.VMEM((3, 16, width), BF16),
            pltpu.VMEM((width, edim), BF16),
            pltpu.VMEM((2, 2, 16, 16, edim), BF16),
            pltpu.VMEM((2, 512, edim), BF16),
            pltpu.VMEM((2, 512, 128), F32),
            pltpu.VMEM((8, 64, edim), BF16),
            pltpu.VMEM((2, 4, 64, edim), BF16),
            pltpu.VMEM((2, 4, 64, edim), BF16),
            pltpu.VMEM((8, 64, edim), BF16),
            pltpu.VMEM((16, 2, 2, 16, 512), F32),
            pltpu.VMEM((3, 8, 128), F32),
            pltpu.VMEM((7, 8, 128), F32),
            dma((4,)), dma((2,)), dma((2,)),
            dma((4,)), dma((4,)), dma((4,)), dma((4,)), dma(()),
            dma((4,)), dma((4,)), dma((4,)), dma((4,)), dma(()),
            dma((4,)), dma((3,)), dma((1,)), dma((1,)), dma((4,)),
            dma((2, 2, 4)), dma(()), dma((2, 2, 4)), dma(()),
            dma((4,)), dma(()), dma(()),
            dma((7,)), dma((3,)),
        ],
        compiler_params=pltpu.CompilerParams(
            collective_id=0, has_side_effects=True, vmem_limit_bytes=50 * 1024 * 1024
        ),
    )(states, gain1, w1, w2, gain2, mapper, jnp.transpose(prompts, (1, 0, 2)), multiplicity.T, sharpness)
    return logit.reshape(1024, 512) - lse.reshape(1024, 128)[:, :1]


def solution(mesh):
    in_specs = (
        P(("img", "cls"), None),
        P(),
        P(None, "cls"),
        P("cls", None),
        P(),
        P(),
        P("cls", "img", None),
        P("cls", None),
        P(),
    )
    out_specs = P("img", "cls")
    return jax.shard_map(shards, mesh=mesh, in_specs=in_specs, out_specs=out_specs, check_vma=False)
```

time: 365 us -> 78.8 us (0.22)
  waiting for transfers between devices: 182 us -> 0 us
  blocking collectives: 127 us -> 0 us
  Pallas kernels: 0 us -> 70.9 us
  matrix products: 20.3 us -> 0 us
  between operations: 15.3 us -> 0.74 us
  other arithmetic: 11.4 us -> 3.13 us
  local copies, waits for them, and re-layouts: 7.98 us -> 3.91 us
    all_gather x2 -> x0, waiting for transfers between devices: 107 us -> none  [the longest x1 57.2 us: shards(): gathered = lax.all_gather(picture_token_states, 'cls', axis=0, tiled=True)]
    reduce_scatter x1 -> x0, waiting for transfers between devices: 74.3 us -> none  [shards(): lax.psum_scatter(rounded_term(jnp.dot(hidden, contracting_linear_map, pre...]
    pallas_call x0 -> x1, Pallas kernels: none -> 70.9 us  [shards(): pl.pallas_call(kernel, name='whole', out_shape=(jax.ShapeDtypeStruct((16,...]
    psum x1 -> x0, blocking collectives: 65.2 us -> none  [shards(): lax.psum(jnp.sum(jnp.exp(category_affinity_values - row_max), axis=1, kee...]
    pmax x1 -> x0, blocking collectives: 62.3 us -> none  [shards(): row_max = lax.pmax(local_max, 'cls')]
    dot_general x4 -> x0, matrix products: 20.3 us -> none  [the longest x1 9.09 us: shards(): jnp.dot(hidden, contracting_linear_map, preferred_element_type=jnp.float32)]
    reduce_sum x7 -> x0, other arithmetic: 8.95 us -> none  [the longest x2 3.66 us: layer_norm(): center = values - jnp.mean(values, axis=-1, keepdims=True)]
  transfers between devices with their start and end apart: 4 -> 0, of which waited for: 3 -> 0; matrix products, arithmetic and copies ran while one was open for 5% -> 0% of each run, Pallas kernels for 0% -> 0%
where the time goes in v1:
time: 78.8 us; the launch traced here: 78.7 us
  Pallas kernels  70.9 us (90%)
  local copies, waits for them, and re-layouts  3.91 us (5%)
  other arithmetic  3.13 us (4%)
    pallas_call x1, Pallas kernels, shards(): pl.pallas_call(kernel, name='whole', out_shape=(jax.ShapeDtypeStruct((16,...  70.9 us
    unnamed x14, local copies, waits for them, and re-layouts  3.91 us
    sub x1, other arithmetic, shards(): return logit.reshape(1024, 512) - lse.reshape(1024, 128)[:, :1]  3.13 us

profile of v1, /device:TPU:1, one launch (start us, length us, event | category | flops | bytes accessed | tf_op | source)
XLA Modules:
  0.0 78.7 jit_solution(9968491756940460616)
XLA Ops:
  0.7 0.0 copy-start
  0.7 0.0 copy-start.1
  0.7 0.0 copy-start.2
  0.7 0.0 copy-start.3
  0.7 0.0 copy-start.4
  0.7 0.0 copy-start.5
  0.7 3.7 %copy.15 = bf16[512,2,1280]{2,0,1:T(8,128)(2,1)} copy(bf16[512,2,1280]{2,1,0:T(2,128)(2,1)} %param.15) | data formatting | bytes 5242880 | tf_op args[6]
  4.4 0.0 copy-done
  4.4 0.0 copy-done.1
  4.4 0.0 copy-done.2
  4.4 0.0 copy-done.3
  4.4 0.0 copy-done.4
  4.5 0.0 copy-done.5
  4.5 70.9 %whole.1 = (f32[16,2,2,16,512]{4,3,2,1,0:T(8,128)}, f32[16,2,2,16,128]{4,3,2,1,0:T(8,128)S(1)}) custom-call(bf16[32,1664]{1,0:T(8,128)(2,1)S(1)} %copy-done.2, f32[1664]{0:T(1024)S(1)} %copy-done.4, bf16[1664,256]{1,0:T(8,128)(2,1)S(1)} %copy-done, bf16[256,1664]{1,0:T(8,128)(2,1)S(1)} %copy-done.1, f32[1664]{0:T(1024)S(1)} %copy-done.5, ...), custom_call_target="tpu_custom_call" | custom-call | tf_op jit(solution)/shard_map/whole/pallas_call | solution.py:346
  75.4 0.2 copy.13
  75.6 3.1 %bitcast_subtract_fusion = f32[1024,512]{1,0:T(8,128)} fusion(f32[16,2,2,16,512]{4,3,2,1,0:T(8,128)} %get-tuple-element.7, f32[1024]{0:T(1024)S(1)} %bitcast.12), kind=kLoop, calls=%fused_computation.1 | loop fusion | flops 524288 | bytes 4198400 | tf_op jit(solution)/shard_map/sub | solution.py:389
Async XLA Ops:
  0.7 3.8 %copy-start = (bf16[1664,256]{1,0:T(8,128)(2,1)S(1)}, bf16[1664,256]{1,0:T(8,128)(2,1)}, u32[]{:S(2)}) copy-start(bf16[1664,256]{1,0:T(8,128)(2,1)} %w1_hbm.1) | copy-start | bytes 2555908
  0.7 3.8 %copy-start.1 = (bf16[256,1664]{1,0:T(8,128)(2,1)S(1)}, bf16[256,1664]{1,0:T(8,128)(2,1)}, u32[]{:S(2)}) copy-start(bf16[256,1664]{1,0:T(8,128)(2,1)} %w2_hbm.1) | copy-start | bytes 2555908
  0.7 3.8 %copy-start.2 = (bf16[32,1664]{1,0:T(8,128)(2,1)S(1)}, bf16[32,1664]{1,0:T(8,128)(2,1)}, u32[]{:S(2)}) copy-start(bf16[32,1664]{1,0:T(8,128)(2,1)} %x_ref.1) | copy-start | bytes 319492
  0.7 3.8 %copy-start.3 = (s32[512,16]{0,1:T(8,128)S(1)}, s32[512,16]{0,1:T(8,128)}, u32[]{:S(2)}) copy-start(s32[512,16]{0,1:T(8,128)} %param.16) | copy-start | bytes 98308
  0.7 3.8 %copy-start.4 = (f32[1664]{0:T(1024)S(1)}, f32[1664]{0:T(1024)}, u32[]{:S(2)}) copy-start(f32[1664]{0:T(1024)} %g1_ref.1) | copy-start | bytes 19972
  0.7 3.8 %copy-start.5 = (f32[1664]{0:T(1024)S(1)}, f32[1664]{0:T(1024)}, u32[]{:S(2)}) copy-start(f32[1664]{0:T(1024)} %g2_ref.1) | copy-start | bytes 19972

commit v2 on v1

v2 whole, which is shorter than its diff:
```python
import jax
import jax.numpy as jnp
from jax import lax
from jax.experimental import pallas as pl
from jax.experimental.pallas import tpu as pltpu
from jax.sharding import PartitionSpec as P

MESH = pl.DeviceIdType.MESH
F32 = jnp.float32
BF16 = jnp.bfloat16
ORDER = (1, 3, 2)


def layer_norm(values, gain):
    center = values - jnp.mean(values, axis=-1, keepdims=True)
    variance = jnp.mean(center * center, axis=-1, keepdims=True)
    return center * lax.rsqrt(variance + 1e-05) * gain


def arrived(ref, sem):
    pltpu.make_async_copy(ref, ref, sem).wait()


class PlaneGather:
    def __init__(self, x, y, at, buf, split, sems):
        self.x, self.y, self.at, self.buf = x, y, at, buf
        self.cols = (pl.ds(0, split), pl.ds(split, buf.shape[-1] - split))
        self.a1, self.a2, self.b1, self.b2, self.out = sems

    def send(self, p, xx, yy, to, sem):
        piece = self.buf.at[xx * 4 + yy, :, self.cols[p]]
        pltpu.make_async_remote_copy(
            src_ref=piece, dst_ref=piece, send_sem=self.out, recv_sem=sem, device_id=to, device_id_type=MESH
        ).start()

    def start(self):
        x, y = self.x, self.y
        for d in ORDER:
            self.send(0, x, y, self.at((x + d) % 4, y), self.a1.at[4 - d])
            self.send(1, x, y, self.at(x, (y + d) % 4), self.b1.at[4 - d])
        for d in ORDER:
            self.send(0, x, y, self.at(x, (y + d) % 4), self.a2.at[0])
            self.send(1, x, y, self.at((x + d) % 4, y), self.b2.at[4 - d])

    def forward(self):
        x, y = self.x, self.y
        for o in ORDER:
            xs, ys = (x + o) % 4, (y + o) % 4
            arrived(self.buf.at[xs * 4 + y, :, self.cols[0]], self.a1.at[o])
            for d in ORDER:
                self.send(0, xs, y, self.at(x, (y + d) % 4), self.a2.at[o])
            arrived(self.buf.at[x * 4 + ys, :, self.cols[1]], self.b1.at[o])
            for d in ORDER:
                self.send(1, x, ys, self.at((x + d) % 4, y), self.b2.at[4 - d])

    def column(self, o):
        arrived(self.buf.at[pl.ds(0, 3), :, self.cols[0]], self.a2.at[o])
        if o:
            arrived(self.buf.at[pl.ds(0, 4), :, self.cols[1]], self.b2.at[o])

    def finish(self):
        arrived(self.buf.at[pl.ds(0, 15)], self.out)


def kernel(
    x_hbm, g1_hbm, w1_hbm, w2_hbm, g2_hbm, map_hbm, tpl_hbm, mult_hbm, sharp_ref,
    lg, lse_out,
    xv, g1v, g2v, multv, tok, w1, w2, part, r1a, r1b, s1a, s1b, r2a, r2b, mapv, emb, tplv, shc, gs, zr, zs, cls,
    lse_mine, lse_in,
    load_sem, w_send, w_recv, g_a1, g_a2, g_b1, g_b2, g_out, e_a1, e_a2, e_b1, e_b2, e_out,
    ra1, rb1, ra2, rb2, rs_out, z_recv, z_out, za_recv, za_out, pair_recv, pair_out, l_recv, l_out,
):
    m = lax.axis_index("cls")
    z = lax.axis_index("img")
    x, y, c = m // 8, (m // 2) % 4, m % 2
    me = x * 4 + y
    width, edim = tok.shape[-1], emb.shape[-1]

    def at(xx, yy, cc=None):
        return (z, (xx * 4 + yy) * 2 + (c if cc is None else cc))

    mate = at(x, y, 1 - c)
    z_up, z_down = ((z + 1) % 8, m), ((z + 7) % 8, m)

    def send(src, dst, s_sem, r_sem, to):
        pltpu.make_async_remote_copy(
            src_ref=src, dst_ref=dst, send_sem=s_sem, recv_sem=r_sem, device_id=to, device_id_type=MESH
        ).start()

    barrier = pltpu.get_barrier_semaphore()
    x_peers = [at((x + d) % 4, y) for d in ORDER]
    x_others = [at((x + d) % 4, y, 1 - c) for d in ORDER]
    y_peers = [at(x, (y + d) % 4) for d in ORDER]
    partners = x_peers + y_peers + [mate, z_up, z_down] + x_others
    for to in partners:
        pl.semaphore_signal(barrier, inc=1, device_id=to, device_id_type=MESH)

    loads = [
        pltpu.make_async_copy(src, dst, load_sem.at[i])
        for i, (src, dst) in enumerate(
            (
                (x_hbm, xv), (g1_hbm, g1v), (mult_hbm, multv), (tpl_hbm, tplv),
                (w1_hbm, w1.at[c]), (w2_hbm, w2.at[c]), (g2_hbm, g2v), (map_hbm, mapv),
            )
        )
    ]
    for load in loads:
        load.start()

    loads[0].wait()
    loads[1].wait()
    states = xv[...].astype(F32)
    normed = layer_norm(states, g1v[...][None, :]).astype(BF16)
    tok[0, me] = normed[:16]
    tok[1, me] = normed[16:]

    loads[2].wait()
    weights = multv[...].astype(F32)
    total = jnp.sum(weights, axis=0, keepdims=True)
    row_id = lax.broadcasted_iota(jnp.int32, weights.shape, 0)
    for t in range(2):
        own = jnp.sum(jnp.where(row_id == 2 * z + t, weights, 0.0), axis=0, keepdims=True)
        portion = own / total
        for q in range(4):
            shc[t, pl.ds(q * 128, 128), :] = jnp.broadcast_to(portion[:, q * 128 : (q + 1) * 128], (128, 128)).T

    pl.semaphore_wait(barrier, len(partners))

    splits = (896, 768)
    gather = [
        PlaneGather(
            x, y, at, tok.at[h], splits[h], (g_a1.at[h], g_a2.at[h], g_b1.at[h], g_b2.at[h], g_out.at[h])
        )
        for h in range(2)
    ]
    gather[0].start()
    send(w1_hbm, w1.at[c], w_send.at[0], w_recv.at[0], mate)
    send(w2_hbm, w2.at[c], w_send.at[1], w_recv.at[1], mate)

    def group_sums(*offsets):
        for off in offsets:
            k = (z + off) % 8

            @pl.loop(0, 2)
            def _(i):
                rows = pl.ds(k * 64 + i * 32, 32)
                acc = None
                for t in range(2):
                    tmpl = tplv[rows, t, :].astype(F32)
                    coef = shc[t, rows, 0:1] * lax.rsqrt(jnp.sum(tmpl * tmpl, axis=-1, keepdims=True) + 1e-06)
                    acc = coef * tmpl if acc is None else acc + coef * tmpl
                gs[k, pl.ds(i * 32, 32), :] = acc.astype(BF16)

    halves = (pl.ds(0, 640), pl.ds(640, 640))

    def z_reduce(s):
        for way, half in ((0, 0), (1, 1), (0, 1), (1, 0)):
            if s == 0 and way != half:
                continue
            cols = halves[half]
            k = (z + 4 + s) % 8 if way == 0 else (z + 4 - s + 8) % 8
            first = s == 0 or (s == 1 and way != half)
            if first:
                src = gs.at[k, :, cols]
            else:
                came = zr.at[way, s - 1, :, cols]
                arrived(came, z_recv.at[way, half, s - 1])
                zs[way, s, :, cols] = (gs[k, :, cols].astype(F32) + came[...].astype(F32)).astype(BF16)
                src = zs.at[way, s, :, cols]
            send(src, zr.at[way, s, :, cols], z_out, z_recv.at[way, half, s], z_down if way == 0 else z_up)

    def z_total():
        for half in range(2):
            cols = halves[half]
            for way in range(2):
                arrived(zr.at[way, 3, :, cols], z_recv.at[way, half, 3])
            cls[z, :, cols] = (
                gs[z, :, cols].astype(F32) + zr[0, 3, :, cols].astype(F32) + zr[1, 3, :, cols].astype(F32)
            ).astype(BF16)

    def z_gather(s):
        for way, half in ((0, 0), (1, 1), (0, 1), (1, 0)):
            cols = halves[half]
            far = 4 if way == half else 3
            k = (z + s) % 8 if way == 0 else (z - s + 8) % 8
            if s > far:
                continue
            chunk = cls.at[k, :, cols]
            if s > 0:
                arrived(chunk, za_recv.at[way, half, s - 1])
            if s < far:
                send(chunk, chunk, za_out, za_recv.at[way, half, s], z_down if way == 0 else z_up)

    def ffn(h):
        for o in range(4):
            gather[h].column(o)
        rows = tok[h].reshape(256, width)
        hidden = []
        for k in range(2):
            pre = jnp.dot(rows, w1[k], preferred_element_type=F32)
            hidden.append((pre * 0.5 * (1.0 + lax.erf(pre * 0.7071067811865476))).astype(BF16))
        out = jnp.dot(hidden[0], w2[0], preferred_element_type=F32)
        out = out + jnp.dot(hidden[1], w2[1], preferred_element_type=F32)
        part[h] = out.astype(BF16).reshape(16, 16, width)
        cols = gather[h].cols
        first = pl.ds(0, splits[h])
        second = pl.ds(0, width - splits[h])
        for o in ORDER + (0,):
            xs = (x + o) % 4
            for d in ORDER:
                yd = (y + d) % 4
                send(
                    part.at[h, xs * 4 + yd, :, cols[0]], r1a.at[h, 3 - d, o, :, first],
                    rs_out.at[h, 0], ra1.at[h, o], at(x, yd),
                )
            if o:
                send(
                    part.at[h, pl.ds(xs * 4, 4), :, cols[1]], r1b.at[h, 3 - o, :, :, second],
                    rs_out.at[h, 1], rb1.at[h, 3 - o], at(xs, y),
                )

    def second_stage(h):
        cols = gather[h].cols
        first = pl.ds(0, splits[h])
        second = pl.ds(0, width - splits[h])
        for o in ORDER:
            xs = (x + o) % 4
            arrived(r1a.at[h, :, o, :, first], ra1.at[h, o])
            total = part[h, xs * 4 + y, :, cols[0]].astype(F32)
            for k in range(3):
                total = total + r1a[h, k, o, :, first].astype(F32)
            s1a[h, o, :, first] = total.astype(BF16)
            send(s1a.at[h, o, :, first], r2a.at[h, 3 - o, :, first], rs_out.at[h, 2], ra2.at[h], at(xs, y))
        for k in range(3):
            arrived(r1b.at[h, k, :, :, second], rb1.at[h, k])
        for o in ORDER:
            ys = (y + o) % 4
            total = part[h, x * 4 + ys, :, cols[1]].astype(F32)
            for k in range(3):
                total = total + r1b[h, k, ys, :, second].astype(F32)
            s1b[h, o, :, second] = total.astype(BF16)
            send(s1b.at[h, o, :, second], r2b.at[h, 3 - o, :, second], rs_out.at[h, 3], rb2.at[h], at(x, ys))

    def embed(h):
        cols = gather[h].cols
        first = pl.ds(0, splits[h])
        second = pl.ds(0, width - splits[h])
        own_a = part[h, me, :, cols[0]].astype(F32)
        own_b = part[h, me, :, cols[1]].astype(F32)
        arrived(r1a.at[h, :, 0, :, first], ra1.at[h, 0])
        for k in range(3):
            own_a = own_a + r1a[h, k, 0, :, first].astype(F32)
            own_b = own_b + r1b[h, k, y, :, second].astype(F32)
        arrived(r2a.at[h, :, :, first], ra2.at[h])
        arrived(r2b.at[h, :, :, second], rb2.at[h])
        for k in range(3):
            own_a = own_a + r2a[h, k, :, first].astype(F32)
            own_b = own_b + r2b[h, k, :, second].astype(F32)
        stream = xv[pl.ds(h * 16, 16), :].astype(F32) + jnp.concatenate([own_a, own_b], axis=1)
        pooled = layer_norm(stream, g2v[...][None, :]).astype(BF16)
        projected = jnp.dot(pooled, mapv[...], preferred_element_type=F32)
        emb[c, h, me] = (
            projected * lax.rsqrt(jnp.sum(projected * projected, axis=-1, keepdims=True) + 1e-06)
        ).astype(BF16)
        spread[h].start()

    spread = [
        PlaneGather(
            x, y, at, emb.at[c, h], edim // 2, (e_a1.at[h], e_a2.at[h], e_b1.at[h], e_b2.at[h], e_out.at[h])
        )
        for h in range(2)
    ]

    def to_mate(h):
        for o in (0, 1, 3, 2):
            spread[h].column(o)
            quad = emb.at[c, h, pl.ds(((x + o) % 4) * 4, 4)]
            send(quad, quad, pair_out.at[h], pair_recv.at[h], mate)

    sharp = sharp_ref[0]

    def logits(core, h):
        rows = emb[core, h].reshape(256, edim)
        classes = cls[...].reshape(512, edim)
        val = sharp * lax.dot_general(rows, classes, (((1,), (1,)), ((), ())), preferred_element_type=F32)
        lg[:, core, h] = val.reshape(16, 16, 512)
        top = jnp.max(val, axis=-1, keepdims=True)
        lse = top + jnp.log(jnp.sum(jnp.exp(val - top), axis=-1, keepdims=True))
        for q in range(2):
            half = jnp.broadcast_to(lse[q * 128 : (q + 1) * 128], (128, 128)).T
            lse_mine[0, pl.ds((h * 2 + core) * 2 + q, 1), :] = half[0:1, :]

    loads[3].wait()
    group_sums(4)
    z_reduce(0)
    gather[0].forward()
    gather[1].start()
    group_sums(5, 3)
    z_reduce(1)
    group_sums(6, 2)
    gather[1].forward()
    group_sums(7, 1, 0)
    z_reduce(2)
    for i in (4, 5, 6, 7):
        loads[i].wait()
    arrived(w1.at[1 - c], w_recv.at[0])
    arrived(w2.at[1 - c], w_recv.at[1])
    ffn(0)
    z_reduce(3)
    ffn(1)
    second_stage(0)
    z_total()
    z_gather(0)
    second_stage(1)
    embed(0)
    z_gather(1)
    spread[0].forward()
    embed(1)
    z_gather(2)
    spread[1].forward()
    to_mate(0)
    z_gather(3)
    z_gather(4)
    logits(c, 0)
    arrived(emb.at[1 - c, 0], pair_recv.at[0])
    logits(1 - c, 0)
    to_mate(1)
    logits(c, 1)
    arrived(emb.at[1 - c, 1], pair_recv.at[1])
    logits(1 - c, 1)

    def merge(values):
        top = values[0]
        for v in values[1:]:
            top = jnp.maximum(top, v)
        acc = jnp.exp(values[0] - top)
        for v in values[1:]:
            acc = acc + jnp.exp(v - top)
        return top + jnp.log(acc)

    for i, d in enumerate(ORDER):
        send(lse_mine.at[0], lse_in.at[4 - d], l_out.at[0], l_recv.at[4 - d], x_peers[i])
        send(lse_mine.at[0], lse_in.at[8 - d], l_out.at[0], l_recv.at[8 - d], x_others[i])
    send(lse_mine.at[0], lse_in.at[0], l_out.at[0], l_recv.at[0], mate)
    for i in range(8):
        if i != 4:
            arrived(lse_in.at[i], l_recv.at[i])
    lse_mine[1] = merge([lse_mine[0]] + [lse_in[i] for i in range(8) if i != 4])
    for i, d in enumerate(ORDER):
        send(lse_mine.at[1], lse_in.at[8 + 4 - d], l_out.at[1], l_recv.at[8 + 4 - d], y_peers[i])

    for h in range(2):
        cols = gather[h].cols
        gather[h].finish()
        spread[h].finish()
        arrived(part.at[h, pl.ds(0, 12), :, cols[0]], rs_out.at[h, 0])
        arrived(part.at[h, pl.ds(0, 12), :, cols[1]], rs_out.at[h, 1])
        arrived(part.at[h, pl.ds(0, 3), :, cols[0]], rs_out.at[h, 2])
        arrived(part.at[h, pl.ds(0, 3), :, cols[1]], rs_out.at[h, 3])
        arrived(emb.at[c, h], pair_out.at[h])
    arrived(w1.at[c], w_send.at[0])
    arrived(w2.at[c], w_send.at[1])
    arrived(gs.at[pl.ds(0, 7)], z_out)
    arrived(gs.at[pl.ds(0, 7)], za_out)
    arrived(lse_in.at[pl.ds(0, 7)], l_out.at[0])

    for d in ORDER:
        arrived(lse_in.at[8 + d], l_recv.at[8 + d])
    lse = merge([lse_mine[1]] + [lse_in[8 + d] for d in ORDER])
    for h in range(2):
        for core in range(2):
            for q in range(2):
                row = (h * 2 + core) * 2 + q
                columns = jnp.broadcast_to(lse[row : row + 1, :], (128, 128)).T
                lse_out[pl.ds(q * 8, 8), core, h] = columns.reshape(8, 16, 128)
    arrived(lse_in.at[pl.ds(0, 3)], l_out.at[1])


def shards(states, gain1, w1, w2, gain2, mapper, prompts, multiplicity, sharpness):
    width = states.shape[1]
    edim = mapper.shape[1]
    hbm = pl.BlockSpec(memory_space=pltpu.HBM)
    vmem = pl.BlockSpec(memory_space=pltpu.VMEM)
    dma = pltpu.SemaphoreType.DMA
    logit, lse = pl.pallas_call(
        kernel,
        name="whole",
        out_shape=(pltpu.VMEM((16, 2, 2, 16, 512), F32), pltpu.VMEM((16, 2, 2, 16, 128), F32)),
        in_specs=[hbm] * 8 + [pl.BlockSpec(memory_space=pltpu.SMEM)],
        out_specs=(vmem, vmem),
        scratch_shapes=[
            pltpu.VMEM((32, width), BF16),
            pltpu.VMEM((width,), F32),
            pltpu.VMEM((width,), F32),
            pltpu.VMEM((16, 512), jnp.int32),
            pltpu.VMEM((2, 16, 16, width), BF16),
            pltpu.VMEM((2, width, 256), BF16),
            pltpu.VMEM((2, 256, width), BF16),
            pltpu.VMEM((2, 16, 16, width), BF16),
            pltpu.VMEM((2, 3, 4, 16, 896), BF16),
            pltpu.VMEM((2, 3, 4, 16, 896), BF16),
            pltpu.VMEM((2, 4, 16, 896), BF16),
            pltpu.VMEM((2, 4, 16, 896), BF16),
            pltpu.VMEM((2, 3, 16, 896), BF16),
            pltpu.VMEM((2, 3, 16, 896), BF16),
            pltpu.VMEM((width, edim), BF16),
            pltpu.VMEM((2, 2, 16, 16, edim), BF16),
            pltpu.VMEM((512, 2, edim), BF16),
            pltpu.VMEM((2, 512, 128), F32),
            pltpu.VMEM((8, 64, edim), BF16),
            pltpu.VMEM((2, 4, 64, edim), BF16),
            pltpu.VMEM((2, 4, 64, edim), BF16),
            pltpu.VMEM((8, 64, edim), BF16),
            pltpu.VMEM((2, 8, 128), F32),
            pltpu.VMEM((12, 8, 128), F32),
            dma((8,)), dma((2,)), dma((2,)),
            dma((2, 4)), dma((2, 4)), dma((2, 4)), dma((2, 4)), dma((2,)),
            dma((2, 4)), dma((2, 4)), dma((2, 4)), dma((2, 4)), dma((2,)),
            dma((2, 4)), dma((2, 3)), dma((2,)), dma((2,)), dma((2, 4)),
            dma((2, 2, 4)), dma(()), dma((2, 2, 4)), dma(()),
            dma((2,)), dma((2,)),
            dma((12,)), dma((2,)),
        ],
        compiler_params=pltpu.CompilerParams(
            collective_id=0, has_side_effects=True, vmem_limit_bytes=61 * 1024 * 1024
        ),
    )(states, gain1, w1, w2, gain2, mapper, prompts, multiplicity.T, sharpness)
    return logit.reshape(1024, 512) - lse.reshape(1024, 128)[:, :1]


def solution(mesh):
    in_specs = (
        P(("img", "cls"), None),
        P(),
        P(None, "cls"),
        P("cls", None),
        P(),
        P(),
        P("cls", "img", None),
        P("cls", None),
        P(),
    )
    out_specs = P("img", "cls")
    return jax.shard_map(shards, mesh=mesh, in_specs=in_specs, out_specs=out_specs, check_vma=False)
```

time: 78.8 us -> 66.1 us (0.84)
  Pallas kernels: 70.9 us -> 63.6 us
  local copies, waits for them, and re-layouts: 3.91 us -> 0.18 us
  other arithmetic: 3.13 us -> 1.54 us
    pallas_call x1, Pallas kernels: 70.9 us -> 63.6 us  [shards(): pl.pallas_call(kernel, name='whole', out_shape=(pltpu.VMEM((16, 2, 2, 16,...]
    unnamed x14 -> x1, local copies, waits for them, and re-layouts: 3.91 us -> 0.18 us
    sub x1, other arithmetic: 3.13 us -> 1.54 us  [shards(): return logit.reshape(1024, 512) - lse.reshape(1024, 128)[:, :1]]
where the time goes in v2:
time: 66.1 us; the launch traced here: 66 us
  Pallas kernels  63.6 us (96%)
  other arithmetic  1.54 us (2%)
    pallas_call x1, Pallas kernels, shards(): pl.pallas_call(kernel, name='whole', out_shape=(pltpu.VMEM((16, 2, 2, 16,...  63.6 us
    sub x1, other arithmetic, shards(): return logit.reshape(1024, 512) - lse.reshape(1024, 128)[:, :1]  1.54 us

profile of v2, /device:TPU:1, one launch (start us, length us, event | category | flops | bytes accessed | tf_op | source)
XLA Modules:
  0.0 66.0 jit_solution(12441239535132767787)
XLA Ops:
  0.7 63.6 %whole.1 = (f32[16,2,2,16,512]{4,3,2,1,0:T(8,128)S(1)}, f32[16,2,2,16,128]{4,3,2,1,0:T(8,128)S(1)}) custom-call(bf16[32,1664]{1,0:T(8,128)(2,1)} %x_hbm.1, f32[1664]{0:T(1024)} %g1_hbm.1, bf16[1664,256]{1,0:T(8,128)(2,1)} %w1_hbm.1, bf16[256,1664]{1,0:T(8,128)(2,1)} %w2_hbm.1, f32[1664]{0:T(1024)} %g2_hbm.1, bf16[1664,1280]{1,0:T(8,128)(2,1)} %map_hbm.1, ...), custom_call_target="tpu_custom_call" | custom-call | tf_op jit(solution)/shard_map/whole/pallas_call | solution.py:385
  64.3 0.2 copy.11
  64.4 1.5 %bitcast_subtract_fusion = f32[1024,512]{1,0:T(8,128)} fusion(f32[16,2,2,16,512]{4,3,2,1,0:T(8,128)S(1)} %get-tuple-element.7, f32[1024]{0:T(1024)S(1)} %bitcast.8), kind=kLoop, calls=%fused_computation | loop fusion | flops 524288 | bytes 4198400 | tf_op jit(solution)/shard_map/sub | solution.py:428

commit v3 on v2

v3 whole, which is shorter than its diff:
```python
import jax
import jax.numpy as jnp
from jax import lax
from jax.experimental import pallas as pl
from jax.experimental.pallas import tpu as pltpu
from jax.sharding import PartitionSpec as P

MESH = pl.DeviceIdType.MESH
F32 = jnp.float32
BF16 = jnp.bfloat16
ORDER = (1, 3, 2)


def layer_norm(values, gain):
    center = values - jnp.mean(values, axis=-1, keepdims=True)
    variance = jnp.mean(center * center, axis=-1, keepdims=True)
    return center * lax.rsqrt(variance + 1e-05) * gain


def arrived(ref, sem):
    pltpu.make_async_copy(ref, ref, sem).wait()


class PlaneGather:
    def __init__(self, u, v, at, buf, sems, relayed):
        self.u, self.v, self.at, self.buf, self.relayed = u, v, at, buf, relayed
        self.first, self.second, self.third, self.out = sems

    def send(self, uu, vv, to, sem):
        piece = self.buf.at[uu * 4 + vv]
        pltpu.make_async_remote_copy(
            src_ref=piece, dst_ref=piece, send_sem=self.out, recv_sem=sem, device_id=to, device_id_type=MESH
        ).start()

    def start(self):
        for d in ORDER:
            self.send(self.u, self.v, self.at((self.u + d) % 4, self.v), self.first.at[4 - d])

    def forward(self, o):
        u, v = self.u, self.v
        uo = (u + o) % 4
        if o:
            arrived(self.buf.at[uo * 4 + v], self.first.at[o])
        self.send(uo, v, self.at(u, (v + 1) % 4), self.second.at[o, 0])
        self.send(uo, v, self.at(u, (v + 3) % 4), self.second.at[o, 1])
        if o not in self.relayed:
            self.send(uo, v, self.at(u, (v + 2) % 4), self.third.at[o])

    def relay(self, o):
        u, v = self.u, self.v
        came, to = (3, 1) if o % 2 == 0 else (1, 3)
        uo, vs = (u + o) % 4, (v + came) % 4
        arrived(self.buf.at[uo * 4 + vs], self.second.at[o, o % 2])
        self.send(uo, vs, self.at(u, (v + to) % 4), self.third.at[o])

    def column(self, o):
        uo = (self.u + o) % 4
        for side, d in ((0, 3), (1, 1)):
            if o not in self.relayed or side != o % 2:
                arrived(self.buf.at[uo * 4 + (self.v + d) % 4], self.second.at[o, side])
        arrived(self.buf.at[uo * 4 + (self.v + 2) % 4], self.third.at[o])

    def finish(self):
        arrived(self.buf.at[pl.ds(0, 15)], self.out)


def kernel(
    x_hbm, g1_hbm, w1_hbm, w2_hbm, g2_hbm, map_hbm, tpl_hbm, mult_hbm, sharp_ref,
    lg, lse_out,
    xv, g1v, g2v, multv, tok, w1, w2, part, r1, s1, r2, mapv, emb, tplv, shc, gs, zr, zs, cls,
    stage, lse_x, lse_y,
    load_sem, w_send, w_recv, g_1, g_2, g_3, g_out, e_1, e_2, e_3, e_out,
    r1_recv, r2_recv, rs_out, z_recv, z_out, za_recv, za_out, pair_recv, pair_out, lg_recv, lg_out, lx_recv, ly_recv, l_out,
):
    m = lax.axis_index("cls")
    z = lax.axis_index("img")
    x, y, c = m // 8, (m // 2) % 4, m % 2
    u, v = x + c * (y - x), y + c * (x - y)
    me = u * 4 + v
    width, edim = tok.shape[-1], emb.shape[-1]

    def device(xx, yy, cc):
        return (z, (xx * 4 + yy) * 2 + cc)

    def at(uu, vv):
        return device(uu + c * (vv - uu), vv + c * (uu - vv), c)

    mate = device(x, y, 1 - c)
    z_up, z_down = ((z + 1) % 8, m), ((z + 7) % 8, m)

    def send(src, dst, s_sem, r_sem, to):
        pltpu.make_async_remote_copy(
            src_ref=src, dst_ref=dst, send_sem=s_sem, recv_sem=r_sem, device_id=to, device_id_type=MESH
        ).start()

    barrier = pltpu.get_barrier_semaphore()
    x_peers = [device((x + d) % 4, y, c) for d in ORDER]
    y_peers = [device(x, (y + d) % 4, c) for d in ORDER]
    y_others = [device(x, (y + d) % 4, 1 - c) for d in ORDER]
    partners = x_peers + y_peers + [mate, z_up, z_down] + y_others
    for to in partners:
        pl.semaphore_signal(barrier, inc=1, device_id=to, device_id_type=MESH)

    loads = [
        pltpu.make_async_copy(src, dst, load_sem.at[i])
        for i, (src, dst) in enumerate(
            (
                (x_hbm, xv), (g1_hbm, g1v), (mult_hbm, multv), (tpl_hbm, tplv),
                (w1_hbm, w1.at[c]), (w2_hbm, w2.at[c]), (g2_hbm, g2v), (map_hbm, mapv),
            )
        )
    ]
    for load in loads:
        load.start()

    loads[0].wait()
    loads[1].wait()
    states = xv[...].astype(F32)
    normed = layer_norm(states, g1v[...][None, :]).astype(BF16)
    tok[0, me] = normed[:16]
    tok[1, me] = normed[16:]

    loads[2].wait()
    weights = multv[...].astype(F32)
    total = jnp.sum(weights, axis=0, keepdims=True)
    row_id = lax.broadcasted_iota(jnp.int32, weights.shape, 0)
    for t in range(2):
        own = jnp.sum(jnp.where(row_id == 2 * z + t, weights, 0.0), axis=0, keepdims=True)
        portion = own / total
        for q in range(4):
            shc[t, pl.ds(q * 128, 128), :] = jnp.broadcast_to(portion[:, q * 128 : (q + 1) * 128], (128, 128)).T

    def group_sums(*offsets):
        for off in offsets:
            k = (z + off) % 8

            @pl.loop(0, 2)
            def _(i):
                rows = pl.ds(k * 64 + i * 32, 32)
                acc = None
                for t in range(2):
                    tmpl = tplv[rows, t, :].astype(F32)
                    coef = shc[t, rows, 0:1] * lax.rsqrt(jnp.sum(tmpl * tmpl, axis=-1, keepdims=True) + 1e-06)
                    acc = coef * tmpl if acc is None else acc + coef * tmpl
                gs[k, pl.ds(i * 32, 32), :] = acc.astype(BF16)

    loads[3].wait()
    group_sums(4)
    pl.semaphore_wait(barrier, len(partners))

    gather = [PlaneGather(u, v, at, tok.at[h], (g_1.at[h], g_2.at[h], g_3.at[h], g_out.at[h]), ()) for h in range(2)]
    halves = (pl.ds(0, 640), pl.ds(640, 640))

    def z_reduce(s):
        for way, half in ((0, 0), (1, 1), (0, 1), (1, 0)):
            if s == 0 and way != half:
                continue
            cols = halves[half]
            k = (z + 4 + s) % 8 if way == 0 else (z + 4 - s + 8) % 8
            first = s == 0 or (s == 1 and way != half)
            if first:
                src = gs.at[k, :, cols]
            else:
                came = zr.at[way, s - 1, :, cols]
                arrived(came, z_recv.at[way, half, s - 1])
                zs[way, s, :, cols] = (gs[k, :, cols].astype(F32) + came[...].astype(F32)).astype(BF16)
                src = zs.at[way, s, :, cols]
            send(src, zr.at[way, s, :, cols], z_out, z_recv.at[way, half, s], z_down if way == 0 else z_up)

    def to_mate(k):
        send(cls.at[c, k], cls.at[c, k], pair_out, pair_recv, mate)

    def z_total():
        for half in range(2):
            cols = halves[half]
            for way in range(2):
                arrived(zr.at[way, 3, :, cols], z_recv.at[way, half, 3])
            cls[c, z, :, cols] = (
                gs[z, :, cols].astype(F32) + zr[0, 3, :, cols].astype(F32) + zr[1, 3, :, cols].astype(F32)
            ).astype(BF16)

    def z_gather(s):
        for way, half in ((0, 0), (1, 1), (0, 1), (1, 0)):
            cols = halves[half]
            far = 4 if way == half else 3
            k = (z + s) % 8 if way == 0 else (z - s + 8) % 8
            if s > far:
                continue
            chunk = cls.at[c, k, :, cols]
            if s > 0:
                arrived(chunk, za_recv.at[way, half, s - 1])
            if s < far:
                send(chunk, chunk, za_out, za_recv.at[way, half, s], z_down if way == 0 else z_up)
        for k in {0: (0,), 4: (4,)}.get(s, (s, 8 - s)):
            to_mate((z + k) % 8)

    def ffn(h):
        for o in range(4):
            gather[h].column(o)
        rows = tok[h].reshape(256, width)
        hidden = []
        for k in range(2):
            pre = jnp.dot(rows, w1[k], preferred_element_type=F32)
            hidden.append((pre * 0.5 * (1.0 + lax.erf(pre * 0.7071067811865476))).astype(BF16))
        out = jnp.dot(hidden[0], w2[0], preferred_element_type=F32)
        out = out + jnp.dot(hidden[1], w2[1], preferred_element_type=F32)
        part[h] = out.astype(BF16).reshape(16, 16, width)

    def first_stage(h):
        for o in ORDER + (0,):
            for d in ORDER:
                vd = (v + d) % 4
                send(
                    part.at[h, ((u + o) % 4) * 4 + vd], r1.at[h, 3 - d, o],
                    rs_out.at[h, 0], r1_recv.at[h, o], at(u, vd),
                )

    def second_stage(h, o):
        uo = (u + o) % 4
        arrived(r1.at[h, :, o], r1_recv.at[h, o])
        total = part[h, uo * 4 + v].astype(F32)
        for k in range(3):
            total = total + r1[h, k, o].astype(F32)
        s1[h, o] = total.astype(BF16)
        send(s1.at[h, o], r2.at[h, 3 - o], rs_out.at[h, 1], r2_recv.at[h], at(uo, v))

    def embed(h):
        total = part[h, me].astype(F32)
        arrived(r1.at[h, :, 0], r1_recv.at[h, 0])
        for k in range(3):
            total = total + r1[h, k, 0].astype(F32)
        arrived(r2.at[h], r2_recv.at[h])
        for k in range(3):
            total = total + r2[h, k].astype(F32)
        stream = xv[pl.ds(h * 16, 16), :].astype(F32) + total
        pooled = layer_norm(stream, g2v[...][None, :]).astype(BF16)
        projected = jnp.dot(pooled, mapv[...], preferred_element_type=F32)
        emb[h, me] = (
            projected * lax.rsqrt(jnp.sum(projected * projected, axis=-1, keepdims=True) + 1e-06)
        ).astype(BF16)

    spread = [PlaneGather(u, v, at, emb.at[h], (e_1.at[h], e_2.at[h], e_3.at[h], e_out.at[h]), ()) for h in range(2)]

    sharp = sharp_ref[0]

    def logits(h):
        for o in range(4):
            spread[h].column(o)
        rows = emb[h].reshape(256, edim)
        vals = []
        for core in (1 - c, c):
            classes = cls[core].reshape(512, edim)
            val = sharp * lax.dot_general(rows, classes, (((1,), (1,)), ((), ())), preferred_element_type=F32)
            for j in range(16):
                uu, vv = j // 4, j % 4
                place = (uu + c * (vv - uu)) * 4 + vv + c * (uu - vv)
                piece = val[j * 16 : (j + 1) * 16]
                if vals:
                    lg[place, c, h] = piece
                else:
                    stage[h, j] = piece
                    send(stage.at[h, j], lg.at[place, c, h], lg_out, lg_recv, mate)
            vals.append(val)
        top = jnp.maximum(jnp.max(vals[0], axis=-1, keepdims=True), jnp.max(vals[1], axis=-1, keepdims=True))
        total = jnp.sum(jnp.exp(vals[0] - top) + jnp.exp(vals[1] - top), axis=-1, keepdims=True)
        lse = top + jnp.log(total)
        for q in range(2):
            half = jnp.broadcast_to(lse[q * 128 : (q + 1) * 128], (128, 128)).T
            lse_x[0, h * 2 + q : h * 2 + q + 1, :] = half[0:1, :]

    z_reduce(0)
    gather[0].start()
    send(w1_hbm, w1.at[c], w_send.at[0], w_recv.at[0], mate)
    send(w2_hbm, w2.at[c], w_send.at[1], w_recv.at[1], mate)
    group_sums(2)
    gather[0].forward(0)
    group_sums(5)
    group_sums(7)
    gather[1].start()
    gather[0].forward(1)
    group_sums(3)
    z_reduce(1)
    gather[0].forward(2)
    gather[0].forward(3)
    group_sums(1)
    group_sums(6)
    gather[1].forward(0)
    gather[1].forward(3)
    gather[1].forward(2)
    gather[1].forward(1)
    group_sums(0)
    z_reduce(2)
    for i in (4, 5, 6, 7):
        loads[i].wait()
    arrived(w1.at[1 - c], w_recv.at[0])
    arrived(w2.at[1 - c], w_recv.at[1])
    ffn(0)
    first_stage(0)
    z_reduce(3)
    ffn(1)
    first_stage(1)
    z_total()
    z_gather(0)
    second_stage(0, 2)
    second_stage(0, 3)
    second_stage(0, 1)
    z_gather(1)
    second_stage(1, 2)
    second_stage(1, 1)
    second_stage(1, 3)
    embed(0)
    spread[0].start()
    spread[0].forward(0)
    z_gather(2)
    embed(1)
    spread[1].start()
    spread[1].forward(0)
    spread[0].forward(2)
    spread[0].forward(1)
    z_gather(3)
    spread[0].forward(3)
    spread[1].forward(2)
    spread[1].forward(3)
    z_gather(4)
    spread[1].forward(1)
    arrived(cls.at[1 - c], pair_recv)
    logits(0)
    logits(1)

    def merge(values):
        top = values[0]
        for v in values[1:]:
            top = jnp.maximum(top, v)
        acc = jnp.exp(values[0] - top)
        for v in values[1:]:
            acc = acc + jnp.exp(v - top)
        return top + jnp.log(acc)

    for i, d in enumerate(ORDER):
        send(lse_x.at[0], lse_x.at[4 - d], l_out.at[0], lx_recv.at[4 - d], x_peers[i])
    for d in ORDER:
        arrived(lse_x.at[d], lx_recv.at[d])
    lse_y[c, 0] = merge([lse_x[i] for i in range(4)])
    mine = lse_y.at[c, 0]
    for i, d in enumerate(ORDER):
        send(mine, lse_y.at[c, 4 - d], l_out.at[1], ly_recv.at[c, 4 - d], y_peers[i])
        send(mine, lse_y.at[c, 4 - d], l_out.at[1], ly_recv.at[c, 4 - d], y_others[i])
    send(mine, mine, l_out.at[1], ly_recv.at[c, 0], mate)

    for h in range(2):
        gather[h].finish()
        spread[h].finish()
        arrived(part.at[h, pl.ds(0, 12)], rs_out.at[h, 0])
        arrived(r2.at[h], rs_out.at[h, 1])
    arrived(w1.at[c], w_send.at[0])
    arrived(w2.at[c], w_send.at[1])
    arrived(gs.at[pl.ds(0, 7)], z_out)
    arrived(gs.at[pl.ds(0, 7)], za_out)
    arrived(cls.at[c], pair_out)
    arrived(stage, lg_out)
    arrived(lse_x.at[pl.ds(0, 3)], l_out.at[0])
    arrived(lg.at[:, 1 - c], lg_recv)

    arrived(lse_y.at[1 - c, 0], ly_recv.at[1 - c, 0])
    for d in ORDER:
        for core in (c, 1 - c):
            arrived(lse_y.at[core, d], ly_recv.at[core, d])
    for core in range(2):
        lse = merge([lse_y[core, i] for i in range(4)])
        for row in range(4):
            columns = jnp.broadcast_to(lse[row : row + 1, :], (128, 128)).T
            for k in range(8):
                j = (row % 2) * 8 + k
                place = (j % 4) * 4 + j // 4 if core else j
                lse_out[place, core, row // 2] = columns[k * 16 : (k + 1) * 16]
    arrived(lse_y.at[0, pl.ds(0, 3)], l_out.at[1])
    arrived(lse_y.at[0], l_out.at[1])


def shards(states, gain1, w1, w2, gain2, mapper, prompts, multiplicity, sharpness):
    width = states.shape[1]
    edim = mapper.shape[1]
    hbm = pl.BlockSpec(memory_space=pltpu.HBM)
    vmem = pl.BlockSpec(memory_space=pltpu.VMEM)
    dma = pltpu.SemaphoreType.DMA
    logit, lse = pl.pallas_call(
        kernel,
        name="whole",
        out_shape=(pltpu.VMEM((16, 2, 2, 16, 512), F32), pltpu.VMEM((16, 2, 2, 16, 128), F32)),
        in_specs=[hbm] * 8 + [pl.BlockSpec(memory_space=pltpu.SMEM)],
        out_specs=(vmem, vmem),
        scratch_shapes=[
            pltpu.VMEM((32, width), BF16),
            pltpu.VMEM((width,), F32),
            pltpu.VMEM((width,), F32),
            pltpu.VMEM((16, 512), jnp.int32),
            pltpu.VMEM((2, 16, 16, width), BF16),
            pltpu.VMEM((2, width, 256), BF16),
            pltpu.VMEM((2, 256, width), BF16),
            pltpu.VMEM((2, 16, 16, width), BF16),
            pltpu.VMEM((2, 3, 4, 16, width), BF16),
            pltpu.VMEM((2, 4, 16, width), BF16),
            pltpu.VMEM((2, 3, 16, width), BF16),
            pltpu.VMEM((width, edim), BF16),
            pltpu.VMEM((2, 16, 16, edim), BF16),
            pltpu.VMEM((512, 2, edim), BF16),
            pltpu.VMEM((2, 512, 128), F32),
            pltpu.VMEM((8, 64, edim), BF16),
            pltpu.VMEM((2, 4, 64, edim), BF16),
            pltpu.VMEM((2, 4, 64, edim), BF16),
            pltpu.VMEM((2, 8, 64, edim), BF16),
            pltpu.VMEM((2, 16, 16, 512), F32),
            pltpu.VMEM((4, 4, 128), F32),
            pltpu.VMEM((2, 4, 4, 128), F32),
            dma((8,)), dma((2,)), dma((2,)),
            dma((2, 4)), dma((2, 4, 2)), dma((2, 4)), dma((2,)),
            dma((2, 4)), dma((2, 4, 2)), dma((2, 4)), dma((2,)),
            dma((2, 4)), dma((2,)), dma((2, 2)),
            dma((2, 2, 4)), dma(()), dma((2, 2, 4)), dma(()),
            dma(()), dma(()), dma(()), dma(()),
            dma((4,)), dma((2, 4)), dma((2,)),
        ],
        compiler_params=pltpu.CompilerParams(
            collective_id=0, has_side_effects=True, vmem_limit_bytes=61 * 1024 * 1024
        ),
    )(states, gain1, w1, w2, gain2, mapper, prompts, multiplicity.T, sharpness)
    return logit.reshape(1024, 512) - lse.reshape(1024, 128)[:, :1]


def solution(mesh):
    in_specs = (
        P(("img", "cls"), None),
        P(),
        P(None, "cls"),
        P("cls", None),
        P(),
        P(),
        P("cls", "img", None),
        P("cls", None),
        P(),
    )
    out_specs = P("img", "cls")
    return jax.shard_map(shards, mesh=mesh, in_specs=in_specs, out_specs=out_specs, check_vma=False)
```

time: 66.1 us -> 64.2 us (0.971)
  Pallas kernels: 63.6 us -> 61.7 us
    pallas_call x1, Pallas kernels: 63.6 us -> 61.7 us  [shards(): pl.pallas_call(kernel, name='whole', out_shape=(pltpu.VMEM((16, 2, 2, 16,...]
where the time goes in v3:
time: 64.2 us; the launch traced here: 64.1 us
  Pallas kernels  61.7 us (96%)
  other arithmetic  1.54 us (2%)
  between operations  0.66 us (1%)
    pallas_call x1, Pallas kernels, shards(): pl.pallas_call(kernel, name='whole', out_shape=(pltpu.VMEM((16, 2, 2, 16,...  61.7 us
    sub x1, other arithmetic, shards(): return logit.reshape(1024, 512) - lse.reshape(1024, 128)[:, :1]  1.54 us

profile of v3, /device:TPU:1, one launch (start us, length us, event | category | flops | bytes accessed | tf_op | source)
XLA Modules:
  0.0 64.1 jit_solution(7815873868265935318)
XLA Ops:
  0.7 61.7 %whole.1 = (f32[16,2,2,16,512]{4,3,2,1,0:T(8,128)S(1)}, f32[16,2,2,16,128]{4,3,2,1,0:T(8,128)S(1)}) custom-call(bf16[32,1664]{1,0:T(8,128)(2,1)} %x_hbm.1, f32[1664]{0:T(1024)} %g1_hbm.1, bf16[1664,256]{1,0:T(8,128)(2,1)} %w1_hbm.1, bf16[256,1664]{1,0:T(8,128)(2,1)} %w2_hbm.1, f32[1664]{0:T(1024)} %g2_hbm.1, bf16[1664,1280]{1,0:T(8,128)(2,1)} %map_hbm.1, ...), custom_call_target="tpu_custom_call" | custom-call | tf_op jit(solution)/shard_map/whole/pallas_call | solution.py:386
  62.4 0.2 copy.11
  62.6 1.5 %bitcast_subtract_fusion = f32[1024,512]{1,0:T(8,128)} fusion(f32[16,2,2,16,512]{4,3,2,1,0:T(8,128)S(1)} %get-tuple-element.7, f32[1024]{0:T(1024)S(1)} %bitcast.8), kind=kLoop, calls=%fused_computation | loop fusion | flops 524288 | bytes 4198400 | tf_op jit(solution)/shard_map/sub | solution.py:427

commit v4 on v3

--- a/solution.py
+++ b/solution.py
@@ -98,9 +98,6 @@
     y_peers = [device(x, (y + d) % 4, c) for d in ORDER]
     y_others = [device(x, (y + d) % 4, 1 - c) for d in ORDER]
     partners = x_peers + y_peers + [mate, z_up, z_down] + y_others
-    for to in partners:
-        pl.semaphore_signal(barrier, inc=1, device_id=to, device_id_type=MESH)
-
     loads = [
         pltpu.make_async_copy(src, dst, load_sem.at[i])
         for i, (src, dst) in enumerate(
@@ -110,7 +107,11 @@
             )
         )
     ]
-    for load in loads:
+    loads[0].start()
+    loads[1].start()
+    for to in partners:
+        pl.semaphore_signal(barrier, inc=1, device_id=to, device_id_type=MESH)
+    for load in loads[2:]:
         load.start()
 
     loads[0].wait()
@@ -119,16 +120,6 @@
     normed = layer_norm(states, g1v[...][None, :]).astype(BF16)
     tok[0, me] = normed[:16]
     tok[1, me] = normed[16:]
-
-    loads[2].wait()
-    weights = multv[...].astype(F32)
-    total = jnp.sum(weights, axis=0, keepdims=True)
-    row_id = lax.broadcasted_iota(jnp.int32, weights.shape, 0)
-    for t in range(2):
-        own = jnp.sum(jnp.where(row_id == 2 * z + t, weights, 0.0), axis=0, keepdims=True)
-        portion = own / total
-        for q in range(4):
-            shc[t, pl.ds(q * 128, 128), :] = jnp.broadcast_to(portion[:, q * 128 : (q + 1) * 128], (128, 128)).T
 
     def group_sums(*offsets):
         for off in offsets:
@@ -144,11 +135,22 @@
                     acc = coef * tmpl if acc is None else acc + coef * tmpl
                 gs[k, pl.ds(i * 32, 32), :] = acc.astype(BF16)
 
-    loads[3].wait()
-    group_sums(4)
     pl.semaphore_wait(barrier, len(partners))
 
     gather = [PlaneGather(u, v, at, tok.at[h], (g_1.at[h], g_2.at[h], g_3.at[h], g_out.at[h]), ()) for h in range(2)]
+    def first_sums():
+        loads[2].wait()
+        weights = multv[...].astype(F32)
+        total = jnp.sum(weights, axis=0, keepdims=True)
+        row_id = lax.broadcasted_iota(jnp.int32, weights.shape, 0)
+        for t in range(2):
+            own = jnp.sum(jnp.where(row_id == 2 * z + t, weights, 0.0), axis=0, keepdims=True)
+            portion = own / total
+            for q in range(4):
+                shc[t, pl.ds(q * 128, 128), :] = jnp.broadcast_to(portion[:, q * 128 : (q + 1) * 128], (128, 128)).T
+        loads[3].wait()
+        group_sums(4)
+
     halves = (pl.ds(0, 640), pl.ds(640, 640))
 
     def z_reduce(s):
@@ -268,27 +270,28 @@
             half = jnp.broadcast_to(lse[q * 128 : (q + 1) * 128], (128, 128)).T
             lse_x[0, h * 2 + q : h * 2 + q + 1, :] = half[0:1, :]
 
+    gather[0].start()
+    first_sums()
     z_reduce(0)
-    gather[0].start()
+    group_sums(3)
+    gather[1].start()
     send(w1_hbm, w1.at[c], w_send.at[0], w_recv.at[0], mate)
     send(w2_hbm, w2.at[c], w_send.at[1], w_recv.at[1], mate)
+    group_sums(6)
+    gather[0].forward(1)
+    gather[0].forward(0)
+    gather[0].forward(3)
+    group_sums(5)
+    gather[0].forward(2)
+    z_reduce(1)
+    group_sums(0)
+    gather[1].forward(3)
+    gather[1].forward(0)
+    group_sums(7)
     group_sums(2)
-    gather[0].forward(0)
-    group_sums(5)
-    group_sums(7)
-    gather[1].start()
-    gather[0].forward(1)
-    group_sums(3)
-    z_reduce(1)
-    gather[0].forward(2)
-    gather[0].forward(3)
-    group_sums(1)
-    group_sums(6)
-    gather[1].forward(0)
-    gather[1].forward(3)
     gather[1].forward(2)
     gather[1].forward(1)
-    group_sums(0)
+    group_sums(1)
     z_reduce(2)
     for i in (4, 5, 6, 7):
         loads[i].wait()
@@ -302,27 +305,27 @@
     z_total()
     z_gather(0)
     second_stage(0, 2)
+    second_stage(0, 1)
+    second_stage(1, 1)
     second_stage(0, 3)
-    second_stage(0, 1)
+    second_stage(1, 3)
     z_gather(1)
     second_stage(1, 2)
-    second_stage(1, 1)
-    second_stage(1, 3)
     embed(0)
     spread[0].start()
     spread[0].forward(0)
     z_gather(2)
+    spread[0].forward(1)
+    spread[0].forward(3)
     embed(1)
     spread[1].start()
+    spread[0].forward(2)
     spread[1].forward(0)
-    spread[0].forward(2)
-    spread[0].forward(1)
     z_gather(3)
-    spread[0].forward(3)
-    spread[1].forward(2)
+    spread[1].forward(1)
     spread[1].forward(3)
     z_gather(4)
-    spread[1].forward(1)
+    spread[1].forward(2)
     arrived(cls.at[1 - c], pair_recv)
     logits(0)
     logits(1)

time: 64.2 us -> 63.9 us (level)
  no operation moved by 1% of the time
where the time goes in v4:
time: 63.9 us; the launch traced here: 63.8 us
  Pallas kernels  61.4 us (96%)
  other arithmetic  1.54 us (2%)
  between operations  0.66 us (1%)
    pallas_call x1, Pallas kernels, shards(): pl.pallas_call(kernel, name='whole', out_shape=(pltpu.VMEM((16, 2, 2, 16,...  61.4 us
    sub x1, other arithmetic, shards(): return logit.reshape(1024, 512) - lse.reshape(1024, 128)[:, :1]  1.54 us

profile of v4, /device:TPU:1, one launch (start us, length us, event | category | flops | bytes accessed | tf_op | source)
XLA Modules:
  0.0 63.8 jit_solution(6097750966813924303)
XLA Ops:
  0.7 61.4 %whole.1 = (f32[16,2,2,16,512]{4,3,2,1,0:T(8,128)S(1)}, f32[16,2,2,16,128]{4,3,2,1,0:T(8,128)S(1)}) custom-call(bf16[32,1664]{1,0:T(8,128)(2,1)} %x_hbm.1, f32[1664]{0:T(1024)} %g1_hbm.1, bf16[1664,256]{1,0:T(8,128)(2,1)} %w1_hbm.1, bf16[256,1664]{1,0:T(8,128)(2,1)} %w2_hbm.1, f32[1664]{0:T(1024)} %g2_hbm.1, bf16[1664,1280]{1,0:T(8,128)(2,1)} %map_hbm.1, ...), custom_call_target="tpu_custom_call" | custom-call | tf_op jit(solution)/shard_map/whole/pallas_call | solution.py:389
  62.1 0.2 copy.11
  62.3 1.5 %bitcast_subtract_fusion = f32[1024,512]{1,0:T(8,128)} fusion(f32[16,2,2,16,512]{4,3,2,1,0:T(8,128)S(1)} %get-tuple-element.7, f32[1024]{0:T(1024)S(1)} %bitcast.8), kind=kLoop, calls=%fused_computation | loop fusion | flops 524288 | bytes 4198400 | tf_op jit(solution)/shard_map/sub | solution.py:430

commit v5 on v3

--- a/solution.py
+++ b/solution.py
@@ -98,9 +98,6 @@
     y_peers = [device(x, (y + d) % 4, c) for d in ORDER]
     y_others = [device(x, (y + d) % 4, 1 - c) for d in ORDER]
     partners = x_peers + y_peers + [mate, z_up, z_down] + y_others
-    for to in partners:
-        pl.semaphore_signal(barrier, inc=1, device_id=to, device_id_type=MESH)
-
     loads = [
         pltpu.make_async_copy(src, dst, load_sem.at[i])
         for i, (src, dst) in enumerate(
@@ -110,7 +107,11 @@
             )
         )
     ]
-    for load in loads:
+    loads[0].start()
+    loads[1].start()
+    for to in partners:
+        pl.semaphore_signal(barrier, inc=1, device_id=to, device_id_type=MESH)
+    for load in loads[2:]:
         load.start()
 
     loads[0].wait()
@@ -119,16 +120,6 @@
     normed = layer_norm(states, g1v[...][None, :]).astype(BF16)
     tok[0, me] = normed[:16]
     tok[1, me] = normed[16:]
-
-    loads[2].wait()
-    weights = multv[...].astype(F32)
-    total = jnp.sum(weights, axis=0, keepdims=True)
-    row_id = lax.broadcasted_iota(jnp.int32, weights.shape, 0)
-    for t in range(2):
-        own = jnp.sum(jnp.where(row_id == 2 * z + t, weights, 0.0), axis=0, keepdims=True)
-        portion = own / total
-        for q in range(4):
-            shc[t, pl.ds(q * 128, 128), :] = jnp.broadcast_to(portion[:, q * 128 : (q + 1) * 128], (128, 128)).T
 
     def group_sums(*offsets):
         for off in offsets:
@@ -144,11 +135,22 @@
                     acc = coef * tmpl if acc is None else acc + coef * tmpl
                 gs[k, pl.ds(i * 32, 32), :] = acc.astype(BF16)
 
-    loads[3].wait()
-    group_sums(4)
     pl.semaphore_wait(barrier, len(partners))
 
     gather = [PlaneGather(u, v, at, tok.at[h], (g_1.at[h], g_2.at[h], g_3.at[h], g_out.at[h]), ()) for h in range(2)]
+    def first_sums():
+        loads[2].wait()
+        weights = multv[...].astype(F32)
+        total = jnp.sum(weights, axis=0, keepdims=True)
+        row_id = lax.broadcasted_iota(jnp.int32, weights.shape, 0)
+        for t in range(2):
+            own = jnp.sum(jnp.where(row_id == 2 * z + t, weights, 0.0), axis=0, keepdims=True)
+            portion = own / total
+            for q in range(4):
+                shc[t, pl.ds(q * 128, 128), :] = jnp.broadcast_to(portion[:, q * 128 : (q + 1) * 128], (128, 128)).T
+        loads[3].wait()
+        group_sums(4)
+
     halves = (pl.ds(0, 640), pl.ds(640, 640))
 
     def z_reduce(s):
@@ -268,8 +270,9 @@
             half = jnp.broadcast_to(lse[q * 128 : (q + 1) * 128], (128, 128)).T
             lse_x[0, h * 2 + q : h * 2 + q + 1, :] = half[0:1, :]
 
+    gather[0].start()
+    first_sums()
     z_reduce(0)
-    gather[0].start()
     send(w1_hbm, w1.at[c], w_send.at[0], w_recv.at[0], mate)
     send(w2_hbm, w2.at[c], w_send.at[1], w_recv.at[1], mate)
     group_sums(2)

time: 64.2 us -> 64.1 us (level)
  no operation moved by 1% of the time
where the time goes in v5:
time: 64.1 us; the launch traced here: 64 us
  Pallas kernels  61.6 us (96%)
  other arithmetic  1.54 us (2%)
  between operations  0.66 us (1%)
    pallas_call x1, Pallas kernels, shards(): pl.pallas_call(kernel, name='whole', out_shape=(pltpu.VMEM((16, 2, 2, 16,...  61.6 us
    sub x1, other arithmetic, shards(): return logit.reshape(1024, 512) - lse.reshape(1024, 128)[:, :1]  1.54 us

profile of v5, /device:TPU:1, one launch (start us, length us, event | category | flops | bytes accessed | tf_op | source)
XLA Modules:
  0.0 64.0 jit_solution(13271588536866545476)
XLA Ops:
  0.7 61.6 %whole.1 = (f32[16,2,2,16,512]{4,3,2,1,0:T(8,128)S(1)}, f32[16,2,2,16,128]{4,3,2,1,0:T(8,128)S(1)}) custom-call(bf16[32,1664]{1,0:T(8,128)(2,1)} %x_hbm.1, f32[1664]{0:T(1024)} %g1_hbm.1, bf16[1664,256]{1,0:T(8,128)(2,1)} %w1_hbm.1, bf16[256,1664]{1,0:T(8,128)(2,1)} %w2_hbm.1, f32[1664]{0:T(1024)} %g2_hbm.1, bf16[1664,1280]{1,0:T(8,128)(2,1)} %map_hbm.1, ...), custom_call_target="tpu_custom_call" | custom-call | tf_op jit(solution)/shard_map/whole/pallas_call | solution.py:389
  62.3 0.2 copy.11
  62.4 1.5 %bitcast_subtract_fusion = f32[1024,512]{1,0:T(8,128)} fusion(f32[16,2,2,16,512]{4,3,2,1,0:T(8,128)S(1)} %get-tuple-element.7, f32[1024]{0:T(1024)S(1)} %bitcast.8), kind=kLoop, calls=%fused_computation | loop fusion | flops 524288 | bytes 4198400 | tf_op jit(solution)/shard_map/sub | solution.py:430
